TPU v7x, 32 devices: a whole 2x2x4 slice. The times are simulated.
32 devices in a mesh: dp: 8 (over y, x, core), tensor: 4 (over z).
Axes of the slice: x: 2, y: 2, z: 4, core: 2. Of those that a mesh axis runs over, the one named last changes fastest.
Arguments:
- tokens: bfloat16 [4096, 768], P('dp'), may hold values from -6 to 6
- encoded: bfloat16 [16384, 768], P('dp'), may hold values from -6 to 6
- cotangent: bfloat16 [4096, 768], P('dp'), may hold values from -6 to 6
- seq_lengths: int32 [32], P('dp'), may hold values from 32 to 256, as said below
- enc_slot: int32 [32], P('dp'), may hold values from 0 to 3, as said below
- buckets: int32 [256], replicated, may hold values from 0 to 31, as said below
- gain_self: float32 [768], replicated, may hold values from 0.25 to 1.75
- gain_cross: float32 [768], replicated, may hold values from 0.25 to 1.75
- gain_ffn: float32 [768], replicated, may hold values from 0.25 to 1.75
- self_query: bfloat16 [768, 768], P(None, 'tensor'), may hold values from -0.02734375 to 0.02734375
- self_key: bfloat16 [768, 768], P(None, 'tensor'), may hold values from -0.21875 to 0.21875
- self_value: bfloat16 [768, 768], P(None, 'tensor'), may hold values from -0.21875 to 0.21875
- self_out: bfloat16 [768, 768], P('tensor'), may hold values from -1.75 to 1.75
- bias_table: bfloat16 [32, 12], P(None, 'tensor'), may hold values from -4 to 4
- cross_query: bfloat16 [768, 768], P(None, 'tensor'), may hold values from -0.02734375 to 0.02734375
- cross_key: bfloat16 [768, 768], P(None, 'tensor'), may hold values from -0.21875 to 0.21875
- cross_value: bfloat16 [768, 768], P(None, 'tensor'), may hold values from -0.21875 to 0.21875
- cross_out: bfloat16 [768, 768], P('tensor'), may hold values from -3.5 to 3.5
- gate_weight: bfloat16 [768, 2048], P(None, 'tensor'), may hold values from -0.21875 to 0.21875
- up_weight: bfloat16 [768, 2048], P(None, 'tensor'), may hold values from -0.21875 to 0.21875
- down_weight: bfloat16 [2048, 768], P('tensor'), may hold values from -0.25 to 0.25
Outputs:
- layer_out: bfloat16 [4096, 768], P('dp')
- grad_tokens: float32 [4096, 768], P('dp')
- grad_encoded: float32 [16384, 768], P('dp', 'tensor')
- grad_gain_self: float32 [768], replicated
- grad_gain_cross: float32 [768], replicated
- grad_gain_ffn: float32 [768], replicated
- grad_self_query: float32 [768, 768], P('dp', 'tensor')
- grad_self_key: float32 [768, 768], P('dp', 'tensor')
- grad_self_value: float32 [768, 768], P('dp', 'tensor')
- grad_self_out: float32 [768, 768], P('tensor', 'dp')
- grad_bias_table: float32 [32, 12], P(None, 'tensor')
- grad_cross_query: float32 [768, 768], P('dp', 'tensor')
- grad_cross_key: float32 [768, 768], P('dp', 'tensor')
- grad_cross_value: float32 [768, 768], P('dp', 'tensor')
- grad_cross_out: float32 [768, 768], P('tensor', 'dp')
- grad_gate_weight: float32 [768, 2048], P('dp', 'tensor')
- grad_up_weight: float32 [768, 2048], P('dp', 'tensor')
- grad_down_weight: float32 [2048, 768], P('tensor', 'dp')
Inputs may be any that keep to these rules, and one draw needn't show every extreme that they name: `seq_lengths`: in each group of 4 entries the lengths sum to at most 512, and the sequences fill their group's rows from the first, in slot order; the rest is padding. In each group one sequence has 256 tokens and another 256 // 8. `enc_slot`: each group of 4 entries is a permutation of 0 to 3. buckets[d] = d for d < 16, never falls as d grows, and is 31 at d = 255.
All inputs are finite; a program needn't handle non-finite values.
Results may differ from a plain program's by a relative error of at most 0.025.
Values may be sent and summed in bfloat16 or wider, within the bound.
A program may use at most 256 MiB of HBM per device.

v0:
```python
from functools import partial

import jax
import jax.numpy as jnp
from jax import lax
from jax.sharding import PartitionSpec as P

HD = 64


eps = 1e-06
masked_score = -1e30
highest = lax.Precision.HIGHEST


def layout(lengths, slots_of, row_count):
    seq_ends = jnp.cumsum(lengths)
    seq_starts = seq_ends - lengths
    where_row = jnp.arange(row_count, dtype=jnp.int32)
    segment = jnp.sum((where_row[:, None] >= seq_ends[None, :]).astype(jnp.int32), axis=1)
    all_starts = jnp.concatenate([seq_starts, seq_ends[-1:]])
    labels = jnp.arange(all_starts.shape[0], dtype=jnp.int32)
    chosen = segment[:, None] == labels[None, :]
    offset = where_row - jnp.sum(jnp.where(chosen, all_starts[None, :], 0), axis=1)
    slot_table = jnp.concatenate([slots_of, jnp.zeros((1,), jnp.int32)])
    row_slot = jnp.sum(jnp.where(chosen, slot_table[None, :], 0), axis=1)
    return (segment, offset, row_slot)


def project(left_side, right_side):
    return jnp.dot(left_side, right_side, preferred_element_type=jnp.float32)


def contract_rows(left_side, right_side):
    return lax.dot_general(
        left_side, right_side, (((0,), (0,)), ((), ())), preferred_element_type=jnp.float32
    )


def contract_cols(left_side, right_side):
    return lax.dot_general(
        left_side, right_side, (((1,), (1,)), ((), ())), preferred_element_type=jnp.float32
    )


def heads_of(operand):
    return operand.reshape(operand.shape[0], -1, HD)


def norm_parts(operand):
    inverse = lax.rsqrt(jnp.mean(operand * operand, axis=-1, keepdims=True) + eps)
    return (operand * inverse, inverse)


def norm_back(grad_normed, gain_vector, scaled, inverse):
    grad_scaled = grad_normed * gain_vector
    return inverse * (grad_scaled - scaled * jnp.mean(grad_scaled * scaled, axis=-1, keepdims=True))


def glu_product(gate_act, up_act):
    return jax.nn.gelu(gate_act, approximate=True) * up_act


def split_blocks(operand, block_size):
    return operand.reshape((operand.shape[0] // block_size, block_size) + operand.shape[1:])


def attend_forward(query_heads, key_heads, value_heads, score_fn, row_info):
    row_count = query_heads.shape[0]
    block_size = min(512, row_count)

    def one_block(block_item):
        q_block, info_block = block_item
        scores = score_fn(q_block, key_heads, info_block)
        row_max = jnp.max(scores, axis=-1, keepdims=True)
        exp_scores = jnp.exp(scores - row_max)
        row_total = jnp.sum(exp_scores, axis=-1, keepdims=True)
        weights = (exp_scores / row_total).astype(jnp.bfloat16)
        result = jnp.einsum(
            "hij,jhd->ihd", weights, value_heads, preferred_element_type=jnp.float32
        )
        return (result, row_max + jnp.log(row_total))

    block_items = (
        split_blocks(query_heads, block_size),
        jax.tree.map(partial(split_blocks, block_size=block_size), row_info),
    )
    result, log_total = lax.map(one_block, block_items)
    return (result.reshape(row_count, -1).astype(jnp.bfloat16), log_total)


def attend_backward(
    query_heads, key_heads, value_heads, grad_out, log_total, score_fn, row_info, bias_fn, bias_init
):
    row_count = query_heads.shape[0]
    block_size = min(512, row_count)
    grad_heads = heads_of(grad_out)

    def one_block(running, block_item):
        grad_keys, grad_values, grad_bias = running
        q_block, info_block, g_block, l_block = block_item
        scores = score_fn(q_block, key_heads, info_block)
        weights = jnp.exp(scores - l_block)
        grad_weights = jnp.einsum(
            "ihd,jhd->hij", g_block, value_heads, preferred_element_type=jnp.float32
        )
        delta_rows = jnp.sum(weights * grad_weights, axis=-1, keepdims=True)
        grad_scores = (weights * (grad_weights - delta_rows)).astype(jnp.bfloat16)
        grad_query = jnp.einsum(
            "hij,jhd->ihd", grad_scores, key_heads, preferred_element_type=jnp.float32
        )
        grad_keys = grad_keys + jnp.einsum(
            "hij,ihd->jhd", grad_scores, q_block, preferred_element_type=jnp.float32
        )
        grad_values = grad_values + jnp.einsum(
            "hij,ihd->jhd",
            weights.astype(jnp.bfloat16),
            g_block,
            preferred_element_type=jnp.float32,
        )
        grad_bias = grad_bias + bias_fn(grad_scores, info_block)
        return ((grad_keys, grad_values, grad_bias), grad_query)

    block_items = (
        split_blocks(query_heads, block_size),
        jax.tree.map(partial(split_blocks, block_size=block_size), row_info),
        split_blocks(grad_heads, block_size),
        log_total,
    )
    zero_keys = jnp.zeros(key_heads.shape, jnp.float32)
    (grad_keys, grad_values, grad_bias), grad_query = lax.scan(
        one_block, (zero_keys, zero_keys, bias_init), block_items
    )
    key_count = key_heads.shape[0]
    return (
        grad_query.reshape(row_count, -1).astype(jnp.bfloat16),
        grad_keys.reshape(key_count, -1).astype(jnp.bfloat16),
        grad_values.reshape(key_count, -1).astype(jnp.bfloat16),
        grad_bias,
    )


def layer_pass(
    hidden_in,
    enc_rows,
    grad_layer,
    segment,
    offset,
    row_slot,
    key_slot,
    buckets,
    weights,
    mixers,
    ffn_hook,
):
    (
        gain_self,
        gain_cross,
        gain_ffn,
        self_query,
        self_key,
        self_value,
        self_out,
        bias_table,
        cross_query,
        cross_key,
        cross_value,
        cross_out,
        gate_weight,
        up_weight,
        down_weight,
    ) = weights
    mix_self, mix_cross, mix_ffn, back_ffn, back_cross, back_self = mixers
    row_count = hidden_in.shape[0]
    span = buckets.shape[0]
    bias_values = bias_table.astype(jnp.float32)
    bucket_labels = jnp.arange(bias_values.shape[0], dtype=jnp.int32)
    bucket_onehot = (buckets[:, None] == bucket_labels[None, :]).astype(jnp.float32)
    distance_table = jnp.dot(
        bucket_onehot, bias_values, precision=highest, preferred_element_type=jnp.float32
    ).T
    steps_back = jnp.arange(span, dtype=jnp.int32)

    def self_scores(q_block, key_heads, info_block):
        seg_block, off_block, row_block = info_block
        distance = jnp.clip(off_block[:, None] - offset[None, :], 0, span - 1)
        allowed = (seg_block[:, None] == segment[None, :]) & (off_block[:, None] >= offset[None, :])
        rel_bias = jnp.take(distance_table, distance, axis=1)
        scores = (
            jnp.einsum("ihd,jhd->hij", q_block, key_heads, preferred_element_type=jnp.float32)
            + rel_bias
        )
        return jnp.where(allowed[None], scores, masked_score)

    def self_bias_grad(grad_scores, info_block):
        seg_block, off_block, row_block = info_block
        columns = jnp.clip(row_block[:, None] - steps_back[None, :], 0, row_count - 1)
        valid = steps_back[None, :] <= off_block[:, None]
        picked = jnp.take_along_axis(grad_scores, columns[None], axis=2)
        return jnp.sum(jnp.where(valid[None], picked.astype(jnp.float32), 0.0), axis=1)

    def cross_scores(q_block, key_heads, info_block):
        allowed = info_block[:, None] == key_slot[None, :]
        scores = jnp.einsum("ihd,jhd->hij", q_block, key_heads, preferred_element_type=jnp.float32)
        return jnp.where(allowed[None], scores, masked_score)

    def no_bias(grad_scores, info_block):
        return jnp.zeros((), jnp.float32)

    scaled_one, inverse_one = norm_parts(hidden_in)
    normed_one = (scaled_one * gain_self).astype(jnp.bfloat16)
    query_self = heads_of(project(normed_one, self_query).astype(jnp.bfloat16))
    key_self = heads_of(project(normed_one, self_key).astype(jnp.bfloat16))
    value_self = heads_of(project(normed_one, self_value).astype(jnp.bfloat16))
    self_info = (segment, offset, jnp.arange(row_count, dtype=jnp.int32))
    attended_self, total_self = attend_forward(
        query_self, key_self, value_self, self_scores, self_info
    )
    after_self = hidden_in + mix_self(project(attended_self, self_out))
    key_cross = heads_of(project(enc_rows, cross_key).astype(jnp.bfloat16))
    value_cross = heads_of(project(enc_rows, cross_value).astype(jnp.bfloat16))
    scaled_two, inverse_two = norm_parts(after_self)
    normed_two = (scaled_two * gain_cross).astype(jnp.bfloat16)
    query_cross = heads_of(project(normed_two, cross_query).astype(jnp.bfloat16))
    attended_cross, total_cross = attend_forward(
        query_cross, key_cross, value_cross, cross_scores, row_slot
    )
    after_cross = after_self + mix_cross(project(attended_cross, cross_out))
    scaled_three, inverse_three = norm_parts(after_cross)
    normed_three = (scaled_three * gain_ffn).astype(jnp.bfloat16)
    gate_act = project(normed_three, gate_weight)
    up_act = project(normed_three, up_weight)
    activated, glu_pullback = jax.vjp(glu_product, gate_act, up_act)
    inner_act = activated.astype(jnp.bfloat16)
    layer_out = after_cross + mix_ffn(project(inner_act, down_weight))
    grad_low = grad_layer.astype(jnp.bfloat16)
    grad_down = contract_rows(inner_act, grad_low)
    grad_inner = contract_cols(grad_low, down_weight)
    grad_gate, grad_up = glu_pullback(grad_inner)
    gate_low = grad_gate.astype(jnp.bfloat16)
    up_low = grad_up.astype(jnp.bfloat16)
    grad_gate_weight = contract_rows(normed_three, gate_low)
    grad_up_weight = contract_rows(normed_three, up_low)
    grad_normed_three = back_ffn(
        contract_cols(gate_low, gate_weight) + contract_cols(up_low, up_weight)
    )
    grad_gain_ffn = jnp.sum(grad_normed_three * scaled_three, axis=0)
    grad_after_cross = grad_layer + norm_back(
        grad_normed_three, gain_ffn, scaled_three, inverse_three
    )
    ffn_grads = ffn_hook(grad_gate_weight, grad_up_weight, grad_down, grad_gain_ffn)
    cross_low = grad_after_cross.astype(jnp.bfloat16)
    grad_cross_out = contract_rows(attended_cross, cross_low)
    grad_attended = contract_cols(cross_low, cross_out).astype(jnp.bfloat16)
    grad_query, grad_keys, grad_values, unused = attend_backward(
        query_cross,
        key_cross,
        value_cross,
        grad_attended,
        total_cross,
        cross_scores,
        row_slot,
        no_bias,
        jnp.zeros((), jnp.float32),
    )
    grad_cross_query = contract_rows(normed_two, grad_query)
    grad_cross_key = contract_rows(enc_rows, grad_keys)
    grad_cross_value = contract_rows(enc_rows, grad_values)
    grad_normed_two, grad_encoded = back_cross(
        contract_cols(grad_query, cross_query),
        contract_cols(grad_keys, cross_key) + contract_cols(grad_values, cross_value),
    )
    grad_gain_cross = jnp.sum(grad_normed_two * scaled_two, axis=0)
    grad_after_self = grad_after_cross + norm_back(
        grad_normed_two, gain_cross, scaled_two, inverse_two
    )
    self_low = grad_after_self.astype(jnp.bfloat16)
    grad_self_out = contract_rows(attended_self, self_low)
    grad_attended = contract_cols(self_low, self_out).astype(jnp.bfloat16)
    bias_init = jnp.zeros((distance_table.shape[0], span), jnp.float32)
    grad_query, grad_keys, grad_values, grad_distance = attend_backward(
        query_self,
        key_self,
        value_self,
        grad_attended,
        total_self,
        self_scores,
        self_info,
        self_bias_grad,
        bias_init,
    )
    grad_bias = jnp.dot(
        bucket_onehot.T, grad_distance.T, precision=highest, preferred_element_type=jnp.float32
    )
    grad_self_query = contract_rows(normed_one, grad_query)
    grad_self_key = contract_rows(normed_one, grad_keys)
    grad_self_value = contract_rows(normed_one, grad_values)
    grad_normed_one = back_self(
        contract_cols(grad_query, self_query)
        + contract_cols(grad_keys, self_key)
        + contract_cols(grad_values, self_value)
    )
    grad_gain_self = jnp.sum(grad_normed_one * scaled_one, axis=0)
    grad_tokens = grad_after_self + norm_back(grad_normed_one, gain_self, scaled_one, inverse_one)
    attention_grads = (
        grad_gain_self,
        grad_gain_cross,
        grad_self_query,
        grad_self_key,
        grad_self_value,
        grad_self_out,
        grad_bias,
        grad_cross_query,
        grad_cross_key,
        grad_cross_value,
        grad_cross_out,
    )
    return (layer_out, grad_tokens, grad_encoded, ffn_grads, attention_grads)


def local(
    tokens,
    encoded,
    cotangent,
    seq_lengths,
    enc_slot,
    buckets,
    gain_self,
    gain_cross,
    gain_ffn,
    self_query,
    self_key,
    self_value,
    self_out,
    bias_table,
    cross_query,
    cross_key,
    cross_value,
    cross_out,
    gate_weight,
    up_weight,
    down_weight,
):
    row_count = tokens.shape[0]
    slot_count = seq_lengths.shape[0]
    enc_span = encoded.shape[0] // slot_count
    data_count = lax.axis_size("dp")
    segment, offset, row_slot = layout(seq_lengths, enc_slot, row_count)
    live_all = (segment < slot_count).astype(jnp.float32)[:, None]

    def spread(vector):
        return jnp.tile(vector.reshape(-1), (data_count,))

    def ffn_hook(grad_gate_weight, grad_up_weight, grad_down, grad_gain_ffn):
        parts = (grad_gate_weight, grad_up_weight, grad_down, grad_gain_ffn)
        return parts

    weights = (
        gain_self,
        gain_cross,
        gain_ffn,
        self_query,
        self_key,
        self_value,
        self_out,
        bias_table,
        cross_query,
        cross_key,
        cross_value,
        cross_out,
        gate_weight,
        up_weight,
        down_weight,
    )
    key_slot = jnp.arange(encoded.shape[0], dtype=jnp.int32) // enc_span
    mixers = (
        lambda operand: lax.psum(operand, "tensor"),
        lambda operand: lax.psum(operand, "tensor"),
        lambda operand: lax.psum(operand.astype(jnp.bfloat16), "tensor").astype(jnp.float32),
        lambda operand: lax.psum(operand, "tensor"),
        lambda first, second: (
            lax.psum(first, "tensor"),
            lax.psum_scatter(
                second.astype(jnp.bfloat16), "tensor", scatter_dimension=1, tiled=True
            ).astype(jnp.float32),
        ),
        lambda operand: lax.psum(operand.astype(jnp.bfloat16), "tensor").astype(jnp.float32),
    )
    layer_full, grad_tokens, grad_encoded, ffn_grads, attention_grads = layer_pass(
        tokens.astype(jnp.float32),
        encoded,
        cotangent.astype(jnp.float32) * live_all,
        segment,
        offset,
        row_slot,
        key_slot,
        buckets,
        weights,
        mixers,
        ffn_hook,
    )
    layer_out = layer_full * live_all
    (
        grad_gain_self,
        grad_gain_cross,
        grad_self_query,
        grad_self_key,
        grad_self_value,
        grad_self_out,
        grad_bias,
        grad_cross_query,
        grad_cross_key,
        grad_cross_value,
        grad_cross_out,
    ) = attention_grads
    bias_shape = grad_bias.shape
    (
        sum_gain_self,
        sum_gain_cross,
        sum_query,
        sum_key,
        sum_value,
        sum_out,
        sum_bias,
        sum_cross_query,
        sum_cross_key,
        sum_cross_value,
        sum_cross_out,
        sum_gate,
        sum_up,
        sum_down,
        sum_gain_ffn,
    ) = (
        lax.psum_scatter(spread(grad_gain_self), "dp", scatter_dimension=0, tiled=True),
        lax.psum_scatter(spread(grad_gain_cross), "dp", scatter_dimension=0, tiled=True),
        lax.psum_scatter(grad_self_query, "dp", scatter_dimension=0, tiled=True),
        lax.psum_scatter(grad_self_key, "dp", scatter_dimension=0, tiled=True),
        lax.psum_scatter(grad_self_value, "dp", scatter_dimension=0, tiled=True),
        lax.psum_scatter(grad_self_out, "dp", scatter_dimension=1, tiled=True),
        lax.psum_scatter(spread(grad_bias), "dp", scatter_dimension=0, tiled=True),
        lax.psum_scatter(grad_cross_query, "dp", scatter_dimension=0, tiled=True),
        lax.psum_scatter(grad_cross_key, "dp", scatter_dimension=0, tiled=True),
        lax.psum_scatter(grad_cross_value, "dp", scatter_dimension=0, tiled=True),
        lax.psum_scatter(grad_cross_out, "dp", scatter_dimension=1, tiled=True),
        lax.psum_scatter(ffn_grads[0], "dp", scatter_dimension=0, tiled=True),
        lax.psum_scatter(ffn_grads[1], "dp", scatter_dimension=0, tiled=True),
        lax.psum_scatter(ffn_grads[2], "dp", scatter_dimension=1, tiled=True),
        lax.psum_scatter(spread(ffn_grads[3]), "dp", scatter_dimension=0, tiled=True),
    )
    sum_bias = sum_bias.reshape(bias_shape)
    return (
        layer_out.astype(jnp.bfloat16),
        grad_tokens,
        grad_encoded,
        sum_gain_self,
        sum_gain_cross,
        sum_gain_ffn,
        sum_query,
        sum_key,
        sum_value,
        sum_out,
        sum_bias,
        sum_cross_query,
        sum_cross_key,
        sum_cross_value,
        sum_cross_out,
        sum_gate,
        sum_up,
        sum_down,
    )


def solution(mesh):
    placed = (
        P("dp", None),
        P("dp", None),
        P("dp", None),
        P("dp"),
        P("dp"),
        P(),
        P(),
        P(),
        P(),
        P(None, "tensor"),
        P(None, "tensor"),
        P(None, "tensor"),
        P("tensor", None),
        P(None, "tensor"),
        P(None, "tensor"),
        P(None, "tensor"),
        P(None, "tensor"),
        P("tensor", None),
        P(None, "tensor"),
        P(None, "tensor"),
        P("tensor", None),
    )
    return jax.shard_map(
        local,
        mesh=mesh,
        in_specs=placed,
        out_specs=(
            P("dp", None),
            P("dp", None),
            P("dp", "tensor"),
            P(),
            P(),
            P(),
            P("dp", "tensor"),
            P("dp", "tensor"),
            P("dp", "tensor"),
            P("tensor", "dp"),
            P(None, "tensor"),
            P("dp", "tensor"),
            P("dp", "tensor"),
            P("dp", "tensor"),
            P("tensor", "dp"),
            P("dp", "tensor"),
            P("dp", "tensor"),
            P("tensor", "dp"),
        ),
        check_vma=False,
    )
```

profile of v0, /device:TPU:0, one launch (start us, length us, event | category | flops | bytes accessed | tf_op | source)
XLA Modules:
  0.0 5196.8 jit_solution(17662779660527909774)
XLA Ops:
  17.1 949.2 %gather_fusion.1 = f32[262144,3]{1,0:T(8,128)} fusion(f32[3,256]{0,1:T(8,128)S(1)} %copy.79, s32[262144]{0:T(1024)} %broadcast_clamp_fusion), kind=kCustom, calls=%fused_computation.clone | custom fusion | bytes 7340032 | tf_op jit(solution)/shard_map/while/body/eval_jaxpr/jit(_take)/gather | solution.py:188
  966.3 71.3 %copy.81 = f32[512,512,3]{0,1,2:T(8,128)} copy(f32[512,512,3]{2,1,0:T(8,128)} %bitcast.7) | data formatting | bytes 6291456 | tf_op jit(solution)/shard_map/while/body/eval_jaxpr/jit(_take)/gather | solution.py:188
  1039.1 2.5 convolution_convert_fusion.12
  1045.9 3.2 fusion.79
  1059.8 65.9 %all-reduce.13.cloned.1.call-done = f32[512,768]{1,0:T(8,128)} async-done(((f32[512,768]{1,0:T(8,128)}), f32[512,768]{1,0:T(8,128)}) %all-reduce.13.cloned.1.call-update) | async-done | bytes 1572880 | tf_op jit(solution)/shard_map/psum | solution.py:377
  1129.7 6.7 select_reduce_fusion.1
  1136.4 7.8 fusion
  1144.3 6.5 fusion.34
  1153.3 68.0 %all-reduce.15.cloned.1.call-done = f32[512,768]{1,0:T(8,128)} async-done(((f32[512,768]{1,0:T(8,128)}), f32[512,768]{1,0:T(8,128)}) %all-reduce.15.cloned.1.call-update) | async-done | bytes 1572880 | tf_op jit(solution)/shard_map/psum | solution.py:378
  1233.0 68.2 %all-reduce.17.cloned.1.call-done = f32[512,768]{1,0:T(8,128)} async-done(((f32[512,768]{1,0:T(8,128)}), f32[512,768]{1,0:T(8,128)}) %all-reduce.17.cloned.1.call-update) | async-done | bytes 1572880 | tf_op jit(solution)/shard_map/psum | solution.py:380
  1301.2 3.1 multiply_reduce_fusion.2
  1308.8 10.5 multiply_reduce_fusion
  1319.3 6.7 multiply_convert_fusion
  1331.5 2.7 convolution_convert_fusion.3
  1334.3 64.3 %all-reduce.19.cloned.1.call-done = f32[512,768]{1,0:T(8,128)} async-done(((f32[512,768]{1,0:T(8,128)}), f32[512,768]{1,0:T(8,128)}) %all-reduce.19.cloned.1.call-update) | async-done | bytes 1572880 | tf_op jit(solution)/shard_map/psum | solution.py:382
  1398.6 3.1 multiply_reduce_fusion.3
  1415.9 9.0 fusion.10
  1425.2 4.9 convolution_convert_fusion.2
  1430.7 4.8 fusion.88
  1435.5 46.1 copy.86
  1481.6 3182.3 %gather_fusion = bf16[131072,3]{1,0:T(8,128)(2,1)} fusion(bf16[3,512,512]{0,2,1:T(8,128)(2,1)} %copy.86, s32[131072]{0:T(1024)} %bitcast.138), kind=kCustom, calls=%fused_computation.1 | custom fusion | bytes 2621440 | tf_op jit(solution)/shard_map/while/body/eval_jaxpr/jit(take_along_axis)/gather | solution.py:199
  4663.9 2.8 convolution_bitcast_fusion.1
  4666.8 43.3 select_reduce_fusion
  4714.6 5.8 add_convert_fusion
  4720.5 3.0 fusion.89
  4723.6 3.1 fusion.90
  4726.8 3.2 fusion.57
  4730.1 2.8 fusion.69
  4733.0 2.7 convolution_bitcast_fusion.3
  4735.7 2.2 copy.100
  4738.0 2.7 convolution_bitcast_fusion.2
  4740.7 2.3 copy.102
  4743.1 2.6 fusion.74
  4745.8 2.6 fusion.72
  4748.5 2.6 fusion.70
  4756.3 2.9 multiply_convert_fusion.2
  4760.8 3.7 all-reduce.21.cloned.1.call-done
  4770.1 58.4 %reduce-scatter.21.cloned.1.call-done = bf16[2048,192]{0,1:T(8,128)(2,1)} async-done(((bf16[2048,768]{0,1:T(8,128)(2,1)}), bf16[2048,192]{0,1:T(8,128)(2,1)}) %reduce-scatter.21.cloned.1.call-update) | async-done | bytes 786448 | tf_op jit(solution)/shard_map/reduce_scatter | solution.py:383
  4828.5 2.5 convert_element_type.247
  4830.9 40.2 reduce-scatter.31.cloned.1.call-done
  4871.1 42.7 reduce-scatter.33.cloned.1.call-done
  4913.8 42.6 reduce-scatter.35.cloned.1.call-done
  4956.3 39.0 reduce-scatter.29.cloned.1.call-done
  4995.3 38.9 reduce-scatter.39.cloned.1.call-done
  5034.2 38.9 reduce-scatter.41.cloned.1.call-done
  5073.1 38.9 reduce-scatter.23.cloned.1.call-done
  5112.0 38.9 reduce-scatter.25.cloned.1.call-done
  5150.9 38.9 reduce-scatter.27.cloned.1.call-done
  (296 shorter events, 84.9 us)
Async XLA Ops:
  7.2 1046.8 %copy-start = (bf16[2048,768]{1,0:T(8,128)(2,1)S(1)}, bf16[2048,768]{1,0:T(8,128)(2,1)}, u32[]{:S(2)}) copy-start(bf16[2048,768]{1,0:T(8,128)(2,1)} %param.24) | copy-start | bytes 9437188
  7.2 6.9 copy-start.81
  7.2 6.9 copy-start.78
  7.2 1118.5 %all-reduce.13.cloned.1.call-start = ((), (), s32[]{:S(2)}) async-start(), calls=%async_computation.12 | async-start | bytes 3145728 | tf_op jit(solution)/shard_map/psum | solution.py:377
  8.3 5.6 copy-start.17
  14.1 1028.6 %copy-start.72 = (f32[512]{0:T(512)}, f32[512]{0:T(512)S(1)}, u32[]{:S(2)}) copy-start(f32[512]{0:T(512)S(1)} %add_rsqrt_fusion.2) | copy-start | bytes 6148
  966.3 72.7 %copy-start.74 = (f32[768]{0:T(1024)S(1)}, f32[768]{0:T(1024)}, u32[]{:S(2)}) copy-start(f32[768]{0:T(1024)} %param.29) | copy-start | bytes 9220
  1039.1 3.7 copy-start.55
  1053.7 167.6 %all-reduce.15.cloned.1.call-start = ((), (), s32[]{:S(2)}) async-start(), calls=%async_computation.13 | async-start | bytes 3145728 | tf_op jit(solution)/shard_map/psum | solution.py:378
  1059.8 69.0 %copy-start.62 = (f32[768]{0:T(1024)S(1)}, f32[768]{0:T(1024)}, u32[]{:S(2)}) copy-start(f32[768]{0:T(1024)} %param.30) | copy-start | bytes 9220
  1136.4 7.8 copy-start.29
  1144.2 7.2 copy-start.33
  1153.0 148.3 %all-reduce.17.cloned.1.call-start = ((), (), s32[]{:S(2)}) async-start(), calls=%async_computation.14 | async-start | bytes 3145728 | tf_op jit(solution)/shard_map/psum | solution.py:380
  1153.3 151.1 %copy-start.69 = (f32[512]{0:T(512)}, f32[512]{0:T(512)S(1)}, u32[]{:S(2)}) copy-start(f32[512]{0:T(512)S(1)} %compare_convert_fusion) | copy-start | bytes 6148
  1153.3 70.2 %copy-start.68 = (f32[768]{0:T(1024)S(1)}, f32[768]{0:T(1024)}, u32[]{:S(2)}) copy-start(f32[768]{0:T(1024)} %param.31) | copy-start | bytes 9220
  1232.9 165.7 %all-reduce.19.cloned.1.call-start = ((), (), s32[]{:S(2)}) async-start(), calls=%async_computation.15 | async-start | bytes 3145728 | tf_op jit(solution)/shard_map/psum | solution.py:382
  1307.7 11.6 copy-start.37
  1307.7 11.6 slice-start
  1308.7 10.5 slice-start.1
  1308.7 10.5 slice-start.2
  1319.3 6.8 copy-start.22
  1330.3 3381.6 %all-reduce.23.cloned.1.call-start = ((), (), s32[]{:S(2)}) async-start(), calls=%async_computation.29 | async-start | bytes 3145728 | tf_op jit(solution)/shard_map/psum | solution.py:379
  1398.6 3.1 copy-start.5
  1398.6 3.1 copy-start.13
  1398.6 3.1 copy-start.63
  1398.6 3.1 copy-start.66
  1411.8 3341.2 %reduce-scatter.43.cloned.1.call-start = ((), (), s32[]{:S(2)}) async-start(), calls=%async_computation.27 | async-start | bytes 884736
  1424.9 5.2 copy-start.76
  1424.9 3329.7 %reduce-scatter.37.cloned.1.call-start = ((), (), s32[]{:S(2)}) async-start(), calls=%async_computation.24 | async-start | bytes 884736
  1481.6 3182.3 %copy-start.41 = (bf16[3,64,512]{2,1,0:T(8,128)(2,1)S(1)}, bf16[3,64,512]{2,1,0:T(8,128)(2,1)}, u32[]{:S(2)}) copy-start(bf16[3,64,512]{2,1,0:T(8,128)(2,1)} %copy-done.40) | copy-start | bytes 589828
  4666.7 97.8 %all-reduce.21.cloned.1.call-start = ((), (), s32[]{:S(2)}) async-start(), calls=%async_computation.28 | async-start | bytes 155648
  4666.7 43.4 copy-start.77
  4666.7 44.0 copy-start.79
  4666.7 45.1 copy-start.73
  4666.8 45.1 copy-start.75
  4714.6 113.9 %reduce-scatter.21.cloned.1.call-start = ((), (), s32[]{:S(2)}) async-start(), calls=%async_computation.16 | async-start | bytes 3932160 | tf_op jit(solution)/shard_map/reduce_scatter | solution.py:383
  4720.4 150.7 %reduce-scatter.31.cloned.1.call-start = ((), (), s32[]{:S(2)}) async-start(), calls=%async_computation.21 | async-start | bytes 1769472 | tf_op jit(solution)/shard_map/reduce_scatter | solution.py:445
  4723.6 3.2 copy-start.70
  4723.6 190.2 %reduce-scatter.33.cloned.1.call-start = ((), (), s32[]{:S(2)}) async-start(), calls=%async_computation.22 | async-start | bytes 1769472 | tf_op jit(solution)/shard_map/reduce_scatter | solution.py:446
  4726.7 3.3 copy-start.64
  4726.7 3.3 copy-start.67
  4726.8 229.6 %reduce-scatter.35.cloned.1.call-start = ((), (), s32[]{:S(2)}) async-start(), calls=%async_computation.23 | async-start | bytes 1769472 | tf_op jit(solution)/shard_map/reduce_scatter | solution.py:447
  4730.0 265.3 %reduce-scatter.29.cloned.1.call-start = ((), (), s32[]{:S(2)}) async-start(), calls=%async_computation.20 | async-start | bytes 884736 | tf_op jit(solution)/shard_map/reduce_scatter | solution.py:441
  4732.9 301.3 %reduce-scatter.39.cloned.1.call-start = ((), (), s32[]{:S(2)}) async-start(), calls=%async_computation.25 | async-start | bytes 884736
  4738.0 335.2 %reduce-scatter.41.cloned.1.call-start = ((), (), s32[]{:S(2)}) async-start(), calls=%async_computation.26 | async-start | bytes 884736
  4743.1 368.9 %reduce-scatter.23.cloned.1.call-start = ((), (), s32[]{:S(2)}) async-start(), calls=%async_computation.17 | async-start | bytes 884736 | tf_op jit(solution)/shard_map/reduce_scatter | solution.py:436
  4745.7 405.1 %reduce-scatter.25.cloned.1.call-start = ((), (), s32[]{:S(2)}) async-start(), calls=%async_computation.18 | async-start | bytes 884736 | tf_op jit(solution)/shard_map/reduce_scatter | solution.py:437
  4748.4 441.4 %reduce-scatter.27.cloned.1.call-start = ((), (), s32[]{:S(2)}) async-start(), calls=%async_computation.19 | async-start | bytes 884736 | tf_op jit(solution)/shard_map/reduce_scatter | solution.py:438
  (56 other events, 103.4 us)
Sparse Core Ops, SparseCore 0:
  1053.9 71.8 all-reduce.12
  1153.1 68.1 all-reduce.14
  1233.0 68.1 all-reduce.16
  1330.4 68.1 all-reduce.18
  1411.9 68.5 all-reduce.22
  1483.5 34.0 reduce-scatter.42
  4666.8 34.1 reduce-scatter.36
  4714.7 49.7 all-reduce.20
  4766.9 61.4 reduce-scatter.20
  4832.5 38.5 reduce-scatter.30
  4875.3 38.4 reduce-scatter.32
  4917.9 38.4 reduce-scatter.34
  4960.4 34.9 reduce-scatter.28
  4999.2 34.9 reduce-scatter.38
  5038.1 34.9 reduce-scatter.40
  5077.0 34.9 reduce-scatter.22
  5115.9 34.9 reduce-scatter.24
  5154.8 34.9 reduce-scatter.26
where the time goes:
time: 5240 us; the launch traced here: 5200 us
  local copies, waits for them, and re-layouts  4280 us (82%)
  waiting for transfers between devices  688 us (13%)
  matrix products  112 us (2%)
  other arithmetic  93.6 us (2%)
    gather x1, local copies, waits for them, and re-layouts, self_bias_grad(): picked = jnp.take_along_axis(grad_scores, columns[None], axis=2)  3180 us
    gather x2, local copies, waits for them, and re-layouts, self_scores(): rel_bias = jnp.take(distance_table, distance, axis=1)  1020 us
    psum x3, waiting for transfers between devices, local(): lax.psum(operand, 'tensor')  202 us
  transfers between devices with their start and end apart: 18, of which 15 were waited for; matrix products, arithmetic and copies ran while one was open for 65% of the time, Pallas kernels for 0%

commit v1 on v0

v1 whole, which is shorter than its diff:
```python
from functools import partial

import jax
import jax.numpy as jnp
from jax import lax
from jax.experimental import pallas as pl
from jax.experimental.pallas import tpu as pltpu
from jax.sharding import PartitionSpec as P

HD = 64


eps = 1e-06
masked_score = -1e30
highest = lax.Precision.HIGHEST


def layout(lengths, slots_of, row_count):
    seq_ends = jnp.cumsum(lengths)
    seq_starts = seq_ends - lengths
    where_row = jnp.arange(row_count, dtype=jnp.int32)
    segment = jnp.sum((where_row[:, None] >= seq_ends[None, :]).astype(jnp.int32), axis=1)
    all_starts = jnp.concatenate([seq_starts, seq_ends[-1:]])
    labels = jnp.arange(all_starts.shape[0], dtype=jnp.int32)
    chosen = segment[:, None] == labels[None, :]
    offset = where_row - jnp.sum(jnp.where(chosen, all_starts[None, :], 0), axis=1)
    slot_table = jnp.concatenate([slots_of, jnp.zeros((1,), jnp.int32)])
    row_slot = jnp.sum(jnp.where(chosen, slot_table[None, :], 0), axis=1)
    return (segment, offset, row_slot)


def project(left_side, right_side):
    return jnp.dot(left_side, right_side, preferred_element_type=jnp.float32)


def contract_rows(left_side, right_side):
    return lax.dot_general(
        left_side, right_side, (((0,), (0,)), ((), ())), preferred_element_type=jnp.float32
    )


def contract_cols(left_side, right_side):
    return lax.dot_general(
        left_side, right_side, (((1,), (1,)), ((), ())), preferred_element_type=jnp.float32
    )


def norm_parts(operand):
    inverse = lax.rsqrt(jnp.mean(operand * operand, axis=-1, keepdims=True) + eps)
    return (operand * inverse, inverse)


def norm_back(grad_normed, gain_vector, scaled, inverse):
    grad_scaled = grad_normed * gain_vector
    return inverse * (grad_scaled - scaled * jnp.mean(grad_scaled * scaled, axis=-1, keepdims=True))


def glu_product(gate_act, up_act):
    return jax.nn.gelu(gate_act, approximate=True) * up_act


def dot_nn(left_side, right_side):
    return jnp.dot(left_side, right_side, preferred_element_type=jnp.float32)


def softmax_parts(scores):
    exp_scores = jnp.exp(scores - jnp.max(scores, axis=-1, keepdims=True))
    return exp_scores / jnp.sum(exp_scores, axis=-1, keepdims=True)


def self_weights(q_head, k_head, table_row, allowed):
    rows, cols = allowed.shape
    bias = pltpu.roll(
        jnp.broadcast_to(table_row, (rows, cols)), 0, 1, stride=1, stride_axis=0
    )
    scores = contract_cols(q_head, k_head) + bias
    return softmax_parts(jnp.where(allowed, scores, masked_score))


def self_allowed(seg_rows, seg_cols):
    shape = (seg_rows.shape[0], seg_cols.shape[1])
    row = lax.broadcasted_iota(jnp.int32, shape, 0)
    col = lax.broadcasted_iota(jnp.int32, shape, 1)
    return (seg_rows == seg_cols) & (col <= row)


def self_forward_kernel(q_ref, k_ref, v_ref, table_ref, seg_rows, seg_cols, out_ref):
    allowed = self_allowed(seg_rows[...], seg_cols[...])
    for head in range(q_ref.shape[1] // HD):
        lanes = slice(head * HD, (head + 1) * HD)
        weights = self_weights(
            q_ref[:, lanes], k_ref[:, lanes], table_ref[head : head + 1, :], allowed
        )
        out_ref[:, lanes] = dot_nn(weights.astype(jnp.bfloat16), v_ref[:, lanes]).astype(
            jnp.bfloat16
        )


def score_grads(weights, grad_weights):
    delta_rows = jnp.sum(weights * grad_weights, axis=-1, keepdims=True)
    return (weights * (grad_weights - delta_rows)).astype(jnp.bfloat16)


def self_backward_kernel(
    q_ref, k_ref, v_ref, table_ref, seg_rows, seg_cols, g_ref, dq_ref, dk_ref, dv_ref, skew_ref
):
    allowed = self_allowed(seg_rows[...], seg_cols[...])
    rows, cols = allowed.shape
    flip = (
        lax.broadcasted_iota(jnp.int32, (cols, cols), 0)
        + lax.broadcasted_iota(jnp.int32, (cols, cols), 1)
        == cols - 1
    ).astype(jnp.float32).astype(jnp.bfloat16)
    for head in range(q_ref.shape[1] // HD):
        lanes = slice(head * HD, (head + 1) * HD)
        q_head, k_head, v_head, g_head = (
            q_ref[:, lanes],
            k_ref[:, lanes],
            v_ref[:, lanes],
            g_ref[:, lanes],
        )
        weights = self_weights(q_head, k_head, table_ref[head : head + 1, :], allowed)
        grad_scores = score_grads(weights, contract_cols(g_head, v_head))
        dq_ref[:, lanes] = dot_nn(grad_scores, k_head).astype(jnp.bfloat16)
        dk_ref[:, lanes] = contract_rows(grad_scores, q_head).astype(jnp.bfloat16)
        dv_ref[:, lanes] = contract_rows(weights.astype(jnp.bfloat16), g_head).astype(
            jnp.bfloat16
        )
        skewed = pltpu.roll(dot_nn(grad_scores, flip), 0, 1, stride=1, stride_axis=0)
        skew_ref[head : head + 1, :] = jnp.sum(skewed, axis=0, keepdims=True)


def slot_masked(operand, slot_rows, slot):
    return jnp.where(slot_rows == slot, operand, jnp.zeros_like(operand))


def slot_cols(left_side, right_ref, lanes, slot_rows, slots):
    span = right_ref.shape[0] // slots
    return sum(
        contract_cols(
            slot_masked(left_side, slot_rows, slot),
            right_ref[slot * span : (slot + 1) * span, lanes],
        )
        for slot in range(slots)
    )


def slot_pick(left_side, right_ref, lanes, slot_rows, slots):
    span = right_ref.shape[0] // slots
    return sum(
        slot_masked(
            dot_nn(left_side, right_ref[slot * span : (slot + 1) * span, lanes]), slot_rows, slot
        )
        for slot in range(slots)
    )


def cross_forward_kernel(slots, q_ref, k_ref, v_ref, slot_ref, out_ref):
    slot_rows = slot_ref[...]
    for head in range(q_ref.shape[1] // HD):
        lanes = slice(head * HD, (head + 1) * HD)
        weights = softmax_parts(slot_cols(q_ref[:, lanes], k_ref, lanes, slot_rows, slots))
        out_ref[:, lanes] = slot_pick(
            weights.astype(jnp.bfloat16), v_ref, lanes, slot_rows, slots
        ).astype(jnp.bfloat16)


def cross_backward_kernel(
    slots, q_ref, k_ref, v_ref, slot_ref, g_ref, dq_ref, dk_ref, dv_ref
):
    slot_rows = slot_ref[...]
    span = k_ref.shape[0] // slots
    for head in range(q_ref.shape[1] // HD):
        lanes = slice(head * HD, (head + 1) * HD)
        q_head, g_head = q_ref[:, lanes], g_ref[:, lanes]
        weights = softmax_parts(slot_cols(q_head, k_ref, lanes, slot_rows, slots))
        grad_scores = score_grads(weights, slot_cols(g_head, v_ref, lanes, slot_rows, slots))
        weights_low = weights.astype(jnp.bfloat16)
        dq_ref[:, lanes] = slot_pick(grad_scores, k_ref, lanes, slot_rows, slots).astype(
            jnp.bfloat16
        )
        for slot in range(slots):
            keys = slice(slot * span, (slot + 1) * span)
            dk_ref[keys, lanes] = contract_rows(
                grad_scores, slot_masked(q_head, slot_rows, slot)
            ).astype(jnp.bfloat16)
            dv_ref[keys, lanes] = contract_rows(
                weights_low, slot_masked(g_head, slot_rows, slot)
            ).astype(jnp.bfloat16)


def run_kernel(body, outs, name, flops, *operands):
    whole = pl.BlockSpec(memory_space=pltpu.VMEM)
    return pl.pallas_call(
        body,
        out_shape=outs,
        in_specs=[whole] * len(operands),
        out_specs=jax.tree.map(lambda leaf: whole, outs),
        compiler_params=pltpu.CompilerParams(vmem_limit_bytes=48 * 1024 * 1024),
        cost_estimate=pl.CostEstimate(flops=flops, bytes_accessed=1 << 22, transcendentals=0),
        name=name,
    )(*operands)


def layer_pass(
    hidden_in,
    enc_rows,
    grad_layer,
    segment,
    row_slot,
    slots,
    buckets,
    weights,
    mixers,
    ffn_hook,
):
    (
        gain_self,
        gain_cross,
        gain_ffn,
        self_query,
        self_key,
        self_value,
        self_out,
        bias_table,
        cross_query,
        cross_key,
        cross_value,
        cross_out,
        gate_weight,
        up_weight,
        down_weight,
    ) = weights
    mix_self, mix_cross, mix_ffn, back_ffn, back_cross, back_self = mixers
    row_count = hidden_in.shape[0]
    span = buckets.shape[0]
    bias_values = bias_table.astype(jnp.float32)
    bucket_labels = jnp.arange(bias_values.shape[0], dtype=jnp.int32)
    bucket_onehot = (buckets[:, None] == bucket_labels[None, :]).astype(jnp.float32)
    distance_table = jnp.dot(
        bucket_onehot, bias_values, precision=highest, preferred_element_type=jnp.float32
    ).T
    back = lax.rem(row_count - jnp.arange(row_count, dtype=jnp.int32), row_count)
    skew_onehot = (back[:, None] == jnp.arange(span, dtype=jnp.int32)[None, :]).astype(jnp.float32)
    skew_table = jnp.dot(
        distance_table, skew_onehot.T, precision=highest, preferred_element_type=jnp.float32
    )
    seg_rows, seg_cols = segment[:, None], segment[None, :]
    slot_rows = row_slot[:, None]

    scaled_one, inverse_one = norm_parts(hidden_in)
    normed_one = (scaled_one * gain_self).astype(jnp.bfloat16)
    query_self = project(normed_one, self_query).astype(jnp.bfloat16)
    key_self = project(normed_one, self_key).astype(jnp.bfloat16)
    value_self = project(normed_one, self_value).astype(jnp.bfloat16)
    low_like = lambda operand: jax.ShapeDtypeStruct(operand.shape, jnp.bfloat16)
    pair_flops = 2 * row_count * row_count * self_query.shape[1]
    attended_self = run_kernel(
        self_forward_kernel,
        low_like(query_self),
        "self_forward",
        8 * pair_flops,
        query_self,
        key_self,
        value_self,
        skew_table,
        seg_rows,
        seg_cols,
    )
    after_self = hidden_in + mix_self(project(attended_self, self_out))
    key_cross = project(enc_rows, cross_key).astype(jnp.bfloat16)
    value_cross = project(enc_rows, cross_value).astype(jnp.bfloat16)
    scaled_two, inverse_two = norm_parts(after_self)
    normed_two = (scaled_two * gain_cross).astype(jnp.bfloat16)
    query_cross = project(normed_two, cross_query).astype(jnp.bfloat16)
    attended_cross = run_kernel(
        partial(cross_forward_kernel, slots),
        low_like(query_cross),
        "cross_forward",
        16 * pair_flops,
        query_cross,
        key_cross,
        value_cross,
        slot_rows,
    )
    after_cross = after_self + mix_cross(project(attended_cross, cross_out))
    scaled_three, inverse_three = norm_parts(after_cross)
    normed_three = (scaled_three * gain_ffn).astype(jnp.bfloat16)
    gate_act = project(normed_three, gate_weight)
    up_act = project(normed_three, up_weight)
    activated, glu_pullback = jax.vjp(glu_product, gate_act, up_act)
    inner_act = activated.astype(jnp.bfloat16)
    layer_out = after_cross + mix_ffn(project(inner_act, down_weight))
    grad_low = grad_layer.astype(jnp.bfloat16)
    grad_down = contract_rows(grad_low, inner_act)
    grad_inner = contract_cols(grad_low, down_weight)
    grad_gate, grad_up = glu_pullback(grad_inner)
    gate_low = grad_gate.astype(jnp.bfloat16)
    up_low = grad_up.astype(jnp.bfloat16)
    grad_gate_weight = contract_rows(normed_three, gate_low)
    grad_up_weight = contract_rows(normed_three, up_low)
    grad_normed_three = back_ffn(
        contract_cols(gate_low, gate_weight) + contract_cols(up_low, up_weight)
    )
    grad_gain_ffn = jnp.sum(grad_normed_three * scaled_three, axis=0)
    grad_after_cross = grad_layer + norm_back(
        grad_normed_three, gain_ffn, scaled_three, inverse_three
    )
    ffn_grads = ffn_hook(grad_gate_weight, grad_up_weight, grad_down, grad_gain_ffn)
    cross_low = grad_after_cross.astype(jnp.bfloat16)
    grad_cross_out = contract_rows(cross_low, attended_cross)
    grad_attended = contract_cols(cross_low, cross_out).astype(jnp.bfloat16)
    grad_query, grad_keys, grad_values = run_kernel(
        partial(cross_backward_kernel, slots),
        (low_like(query_cross), low_like(key_cross), low_like(value_cross)),
        "cross_backward",
        32 * pair_flops,
        query_cross,
        key_cross,
        value_cross,
        slot_rows,
        grad_attended,
    )
    grad_cross_query = contract_rows(normed_two, grad_query)
    grad_cross_key = contract_rows(enc_rows, grad_keys)
    grad_cross_value = contract_rows(enc_rows, grad_values)
    grad_normed_two, grad_encoded = back_cross(
        contract_cols(grad_query, cross_query),
        contract_cols(grad_keys, cross_key) + contract_cols(grad_values, cross_value),
    )
    grad_gain_cross = jnp.sum(grad_normed_two * scaled_two, axis=0)
    grad_after_self = grad_after_cross + norm_back(
        grad_normed_two, gain_cross, scaled_two, inverse_two
    )
    self_low = grad_after_self.astype(jnp.bfloat16)
    grad_self_out = contract_rows(self_low, attended_self)
    grad_attended = contract_cols(self_low, self_out).astype(jnp.bfloat16)
    grad_query, grad_keys, grad_values, grad_skew = run_kernel(
        self_backward_kernel,
        (
            low_like(query_self),
            low_like(key_self),
            low_like(value_self),
            jax.ShapeDtypeStruct(skew_table.shape, jnp.float32),
        ),
        "self_backward",
        32 * pair_flops,
        query_self,
        key_self,
        value_self,
        skew_table,
        seg_rows,
        seg_cols,
        grad_attended,
    )
    grad_distance = jnp.roll(grad_skew, 1, axis=1)[:, :span]
    grad_bias = jnp.dot(
        bucket_onehot.T, grad_distance.T, precision=highest, preferred_element_type=jnp.float32
    )
    grad_self_query = contract_rows(normed_one, grad_query)
    grad_self_key = contract_rows(normed_one, grad_keys)
    grad_self_value = contract_rows(normed_one, grad_values)
    grad_normed_one = back_self(
        contract_cols(grad_query, self_query)
        + contract_cols(grad_keys, self_key)
        + contract_cols(grad_values, self_value)
    )
    grad_gain_self = jnp.sum(grad_normed_one * scaled_one, axis=0)
    grad_tokens = grad_after_self + norm_back(grad_normed_one, gain_self, scaled_one, inverse_one)
    attention_grads = (
        grad_gain_self,
        grad_gain_cross,
        grad_self_query,
        grad_self_key,
        grad_self_value,
        grad_self_out,
        grad_bias,
        grad_cross_query,
        grad_cross_key,
        grad_cross_value,
        grad_cross_out,
    )
    return (layer_out, grad_tokens, grad_encoded, ffn_grads, attention_grads)


def local(
    tokens,
    encoded,
    cotangent,
    seq_lengths,
    enc_slot,
    buckets,
    gain_self,
    gain_cross,
    gain_ffn,
    self_query,
    self_key,
    self_value,
    self_out,
    bias_table,
    cross_query,
    cross_key,
    cross_value,
    cross_out,
    gate_weight,
    up_weight,
    down_weight,
):
    row_count = tokens.shape[0]
    slot_count = seq_lengths.shape[0]
    segment, offset, row_slot = layout(seq_lengths, enc_slot, row_count)
    live_all = (segment < slot_count).astype(jnp.float32)[:, None]

    def ffn_hook(grad_gate_weight, grad_up_weight, grad_down, grad_gain_ffn):
        parts = (grad_gate_weight, grad_up_weight, grad_down, grad_gain_ffn)
        return parts

    weights = (
        gain_self,
        gain_cross,
        gain_ffn,
        self_query,
        self_key,
        self_value,
        self_out,
        bias_table,
        cross_query,
        cross_key,
        cross_value,
        cross_out,
        gate_weight,
        up_weight,
        down_weight,
    )
    def sum_tensor(operand):
        return lax.psum(operand.astype(jnp.bfloat16), "tensor").astype(jnp.float32)

    mixers = (
        sum_tensor,
        sum_tensor,
        sum_tensor,
        sum_tensor,
        lambda first, second: (
            sum_tensor(first),
            lax.psum_scatter(
                second.astype(jnp.bfloat16), "tensor", scatter_dimension=1, tiled=True
            ).astype(jnp.float32),
        ),
        sum_tensor,
    )
    layer_full, grad_tokens, grad_encoded, ffn_grads, attention_grads = layer_pass(
        tokens.astype(jnp.float32),
        encoded,
        cotangent.astype(jnp.float32) * live_all,
        segment,
        row_slot,
        slot_count,
        buckets,
        weights,
        mixers,
        ffn_hook,
    )
    layer_out = layer_full * live_all
    (
        grad_gain_self,
        grad_gain_cross,
        grad_self_query,
        grad_self_key,
        grad_self_value,
        grad_self_out,
        grad_bias,
        grad_cross_query,
        grad_cross_key,
        grad_cross_value,
        grad_cross_out,
    ) = attention_grads
    bias_shape = grad_bias.shape
    grad_gate, grad_up, grad_down, grad_gain_ffn = ffn_grads

    def sum_rows(parts):
        joined = jnp.concatenate([part.astype(jnp.bfloat16) for part in parts], axis=1)
        summed = lax.psum_scatter(joined, "dp", scatter_dimension=0, tiled=True).astype(jnp.float32)
        ends = [sum(part.shape[1] for part in parts[: at + 1]) for at in range(len(parts))]
        return jnp.split(summed, ends[:-1], axis=1)

    sum_gate, sum_up, sum_down = sum_rows((grad_gate, grad_up, grad_down))
    sum_cross_query, sum_cross_key, sum_cross_value, sum_cross_out = sum_rows(
        (grad_cross_query, grad_cross_key, grad_cross_value, grad_cross_out)
    )
    sum_query, sum_key, sum_value, sum_out = sum_rows(
        (grad_self_query, grad_self_key, grad_self_value, grad_self_out)
    )
    sum_out, sum_cross_out, sum_down = sum_out.T, sum_cross_out.T, sum_down.T
    small = jnp.concatenate(
        [grad_gain_self, grad_gain_cross, grad_gain_ffn, grad_bias.reshape(-1)]
    )
    sum_gain_self, sum_gain_cross, sum_gain_ffn, sum_bias = jnp.split(
        lax.psum(small, "dp"), [width * grad_gain_self.shape[0] for width in (1, 2, 3)]
    )
    sum_bias = sum_bias.reshape(bias_shape)
    return (
        layer_out.astype(jnp.bfloat16),
        grad_tokens,
        grad_encoded,
        sum_gain_self,
        sum_gain_cross,
        sum_gain_ffn,
        sum_query,
        sum_key,
        sum_value,
        sum_out,
        sum_bias,
        sum_cross_query,
        sum_cross_key,
        sum_cross_value,
        sum_cross_out,
        sum_gate,
        sum_up,
        sum_down,
    )


def solution(mesh):
    placed = (
        P("dp", None),
        P("dp", None),
        P("dp", None),
        P("dp"),
        P("dp"),
        P(),
        P(),
        P(),
        P(),
        P(None, "tensor"),
        P(None, "tensor"),
        P(None, "tensor"),
        P("tensor", None),
        P(None, "tensor"),
        P(None, "tensor"),
        P(None, "tensor"),
        P(None, "tensor"),
        P("tensor", None),
        P(None, "tensor"),
        P(None, "tensor"),
        P("tensor", None),
    )
    return jax.shard_map(
        local,
        mesh=mesh,
        in_specs=placed,
        out_specs=(
            P("dp", None),
            P("dp", None),
            P("dp", "tensor"),
            P(),
            P(),
            P(),
            P("dp", "tensor"),
            P("dp", "tensor"),
            P("dp", "tensor"),
            P("tensor", "dp"),
            P(None, "tensor"),
            P("dp", "tensor"),
            P("dp", "tensor"),
            P("dp", "tensor"),
            P("tensor", "dp"),
            P("dp", "tensor"),
            P("dp", "tensor"),
            P("tensor", "dp"),
        ),
        check_vma=False,
    )
```

time: 5240 us -> 526 us (0.10)
  local copies, waits for them, and re-layouts: 4280 us -> 43 us
  waiting for transfers between devices: 688 us -> 349 us
  matrix products: 112 us -> 40.9 us
  other arithmetic: 93.6 us -> 22.6 us
    gather x3 -> x0, local copies, waits for them, and re-layouts: 4200 us -> none  [the longest x1 3180 us: self_bias_grad(): picked = jnp.take_along_axis(grad_scores, columns[None], axis=2)]
    reduce_scatter x7 -> x0, waiting for transfers between devices: 281 us -> none  [the longest x1 42.7 us: local(): lax.psum_scatter(ffn_grads[1], 'dp', scatter_dimension=0, tiled=True)]
  transfers between devices with their start and end apart: 18 -> 9, of which waited for: 15 -> 9; matrix products, arithmetic and copies ran while one was open for 65% -> 10% of each run, Pallas kernels for 0% -> 1%
where the time goes in v1:
time: 526 us; the launch traced here: 517 us
  waiting for transfers between devices  349 us (66%)
  local copies, waits for them, and re-layouts  43 us (8%)
  matrix products  40.9 us (8%)
  blocking collectives  22.9 us (4%)
  other arithmetic  22.6 us (4%)
  Pallas kernels  22.5 us (4%)
  between operations  14.9 us (3%)
    psum x5, waiting for transfers between devices, sum_tensor(): return lax.psum(operand.astype(jnp.bfloat16), 'tensor').astype(jnp.float32)  229 us
    unnamed x12, waiting for transfers between devices  63 us
    reduce_scatter x1, waiting for transfers between devices, local(): lax.psum_scatter(second.astype(jnp.bfloat16), 'tensor', scatter_dimension...  56.9 us
    unnamed x166, local copies, waits for them, and re-layouts  35.9 us
    psum x1, blocking collectives, local(): lax.psum(small, 'dp')  22.9 us
    pallas_call x4, Pallas kernels, run_kernel(): pl.pallas_call(body, out_shape=outs, in_specs=[whole] * len(operands), ou...  22.5 us
    dot_general x11, matrix products, project(): return jnp.dot(left_side, right_side, preferred_element_type=jnp.float32)  17.6 us
    dot_general x11, matrix products, contract_cols(): lax.dot_general(left_side, right_side, (((1,), (1,)), ((), ())), preferre...  12.7 us
  transfers between devices with their start and end apart: 9, of which 9 were waited for; matrix products, arithmetic and copies ran while one was open for 10% of the time, Pallas kernels for 1%

profile of v1, /device:TPU:0, one launch (start us, length us, event | category | flops | bytes accessed | tf_op | source)
XLA Modules:
  0.0 516.8 jit_solution(15853983759874056231)
XLA Ops:
  8.3 1.4 fusion.22
  9.8 2.3 convolution_convert_fusion.18.v_ref
  19.7 4.3 self_forward.1
  24.1 1.2 convolution_convert_fusion.8
  26.4 3.0 convolution_convert_fusion.1.k_ref
  29.5 2.0 convolution_convert_fusion.v_ref
  31.4 40.4 %all-reduce.7.cloned.1.call-done = bf16[512,768]{1,0:T(8,128)(2,1)} async-done(((bf16[512,768]{1,0:T(8,128)(2,1)}), bf16[512,768]{1,0:T(8,128)(2,1)}) %all-reduce.7.cloned.1.call-update) | async-done | bytes 786448 | tf_op jit(solution)/shard_map/psum | solution.py:436
  71.8 1.8 multiply_reduce_fusion.1
  73.7 1.6 convolution_convert_fusion.17.q_ref
  75.4 4.3 cross_forward.1
  80.5 1.2 convolution_convert_fusion.7
  82.1 42.7 %all-reduce.9.cloned.1.call-done = bf16[512,768]{1,0:T(8,128)(2,1)} async-done(((bf16[512,768]{1,0:T(8,128)(2,1)}), bf16[512,768]{1,0:T(8,128)(2,1)}) %all-reduce.9.cloned.1.call-update) | async-done | bytes 786448 | tf_op jit(solution)/shard_map/psum | solution.py:436
  124.9 2.0 multiply_reduce_fusion
  127.2 1.5 copy-done.44
  131.4 2.1 multiply_convert_fusion.3
  134.6 1.5 add_convert_fusion.2
  136.1 2.8 convolution_convert_fusion.6
  139.0 40.3 %all-reduce.11.cloned.1.call-done = bf16[512,768]{1,0:T(8,128)(2,1)} async-done(((bf16[512,768]{1,0:T(8,128)(2,1)}), bf16[512,768]{1,0:T(8,128)(2,1)}) %all-reduce.11.cloned.1.call-update) | async-done | bytes 786448 | tf_op jit(solution)/shard_map/psum | solution.py:436
  179.2 2.4 fusion.17
  181.7 1.7 fusion.16
  185.6 1.8 copy.136.g_ref
  189.3 1.2 copy-done.16
  190.5 1.2 copy-done.18
  192.7 9.2 %cross_backward.1 = (bf16[512,192]{1,0:T(8,128)(2,1)S(1)}, bf16[2048,192]{1,0:T(8,128)(2,1)S(1)}, bf16[2048,192]{1,0:T(8,128)(2,1)S(1)}) custom-call(bf16[512,192]{1,0:T(8,128)(2,1)S(1)} %copy-done.20, bf16[2048,192]{1,0:T(8,128)(2,1)S(1)} %copy-done.16, bf16[2048,192]{1,0:T(8,128)(2,1)S(1)} %copy-done.18, s32[512,1]{1,0:T(8,128)S(1)} %copy-done.12, ...), custom_call_target="tpu_custom_call" | custom-call | flops 3221225472 | bytes 4194304 | tf_op jit(solution)/shard_map/cross_backward/pallas_call | solution.py:194
  201.9 1.6 fusion.25
  203.5 1.2 convolution_convert_fusion.5
  205.0 1.9 convolution_convert_fusion.11
  209.3 1.5 copy.159
  210.8 37.1 %all-reduce.13.cloned.1.call-done = bf16[512,768]{1,0:T(8,128)(2,1)} async-done(((bf16[512,768]{1,0:T(8,128)(2,1)}), bf16[512,768]{1,0:T(8,128)(2,1)}) %all-reduce.13.cloned.1.call-update) | async-done | bytes 786448 | tf_op jit(solution)/shard_map/psum | solution.py:436
  247.9 2.0 fusion.18
  252.8 4.7 self_backward.1
  258.9 1.2 add_convert_fusion.1
  262.7 1.5 copy.157
  265.1 1.8 convolution_convert_fusion.4
  267.8 2.5 copy.161
  270.3 1.2 copy-done.3
  272.6 2.7 add_convert_fusion
  275.8 11.3 %reduce-scatter.15.cloned.1.call-done = bf16[96,768]{1,0:T(8,128)(2,1)} async-done(((bf16[768,768]{1,0:T(8,128)(2,1)}), bf16[96,768]{1,0:T(8,128)(2,1)}) %reduce-scatter.15.cloned.1.call-update) | async-done | bytes 147472
  291.1 68.5 %all-reduce.15.cloned.1.call-done = (bf16[512,768]{1,0:T(8,128)(2,1)}, bf16[512,768]{1,0:T(8,128)(2,1)}) async-done(((bf16[512,768]{1,0:T(8,128)(2,1)}, bf16[512,768]{1,0:T(8,128)(2,1)}), (bf16[512,768]{1,0:T(8,128)(2,1)}, bf16[512,768]{1,0:T(8,128)(2,1)})) %all-reduce.15.cloned.1.call-update) | async-done | bytes 1572880 | tf_op jit(solution)/shard_map/psum | solution.py:436
  359.6 1.9 fusion.21
  361.5 22.9 %psum.55 = f32[2400]{0:T(1024)S(1)} all-reduce(f32[2400]{0:T(1024)S(1)} %pad_maximum_fusion.3), channel_id=1, replica_groups=mesh['dp'=8,'tensor'=4] {'dp'}, use_global_device_ids=true, to_apply=%region_19.20 | all-reduce | flops 2400 | bytes 19200 | tf_op jit(solution)/shard_map/psum | solution.py:498
  385.7 3.6 fusion.10
  389.3 9.7 %reduce-scatter.13.cloned.1.call-done = bf16[96,768]{1,0:T(8,128)(2,1)} async-done(((bf16[768,768]{1,0:T(8,128)(2,1)}), bf16[96,768]{1,0:T(8,128)(2,1)}) %reduce-scatter.13.cloned.1.call-update) | async-done | bytes 147472
  403.0 41.9 %reduce-scatter.17.cloned.1.call-done = bf16[96,1536]{1,0:T(8,128)(2,1)} async-done(((bf16[768,1536]{1,0:T(8,128)(2,1)}), bf16[96,1536]{1,0:T(8,128)(2,1)}) %reduce-scatter.17.cloned.1.call-update) | async-done | bytes 294928
  444.9 1.2 copy.162
  448.7 1.2 slice_bitcast_fusion
  450.6 56.9 %reduce-scatter.11.cloned.1.call-done = bf16[2048,192]{0,1:T(8,128)(2,1)} async-done(((bf16[2048,768]{0,1:T(8,128)(2,1)}), bf16[2048,192]{0,1:T(8,128)(2,1)}) %reduce-scatter.11.cloned.1.call-update) | async-done | bytes 786448 | tf_op jit(solution)/shard_map/reduce_scatter | solution.py:445
  507.6 2.5 convert_element_type.198
  (231 shorter events, 45.6 us)
Async XLA Ops:
  7.2 19.3 %copy-start = (bf16[2048,768]{1,0:T(8,128)(2,1)S(1)}, bf16[2048,768]{1,0:T(8,128)(2,1)}, u32[]{:S(2)}) copy-start(bf16[2048,768]{1,0:T(8,128)(2,1)} %param.22) | copy-start | bytes 9437188
  7.2 4.9 copy-start.68
  7.2 64.6 %all-reduce.7.cloned.1.call-start = ((), (), s32[]{:S(2)}) async-start(), calls=%async_computation.4 | async-start | bytes 1572864 | tf_op jit(solution)/shard_map/psum | solution.py:436
  8.3 3.9 copy-start.30
  8.3 3.9 copy-start.61
  13.3 2.0 copy-start.71
  13.3 2.0 copy-start.72
  19.7 4.3 copy-start.50
  25.3 99.6 %all-reduce.9.cloned.1.call-start = ((), (), s32[]{:S(2)}) async-start(), calls=%async_computation.5 | async-start | bytes 1572864 | tf_op jit(solution)/shard_map/psum | solution.py:436
  26.4 3.0 copy-start.65
  31.4 42.3 %copy-start.69 = (f32[768]{0:T(1024)S(1)}, f32[768]{0:T(1024)}, u32[]{:S(2)}) copy-start(f32[768]{0:T(1024)} %param.28) | copy-start | bytes 9220
  71.8 1.9 copy-start.31
  71.8 1.9 copy-start.38
  73.7 1.7 copy-start.11
  73.7 1.7 copy-start.15
  73.7 1.7 copy-start.17
  75.4 4.3 copy-start.19
  75.4 5.1 copy-start.48
  81.7 97.5 %all-reduce.11.cloned.1.call-start = ((), (), s32[]{:S(2)}) async-start(), calls=%async_computation.6 | async-start | bytes 1572864 | tf_op jit(solution)/shard_map/psum | solution.py:436
  82.1 44.8 %copy-start.67 = (f32[768]{0:T(1024)S(1)}, f32[768]{0:T(1024)}, u32[]{:S(2)}) copy-start(f32[768]{0:T(1024)} %param.29) | copy-start | bytes 9220
  126.9 2.3 copy-start.27
  126.9 1.7 copy-start.44
  136.1 111.8 %all-reduce.13.cloned.1.call-start = ((), (), s32[]{:S(2)}) async-start(), calls=%async_computation.7 | async-start | bytes 1572864 | tf_op jit(solution)/shard_map/psum | solution.py:436
  179.2 2.4 copy-start.28
  179.2 2.4 copy-start.47
  181.7 2.9 copy-start.49
  204.7 82.4 %reduce-scatter.15.cloned.1.call-start = ((), (), s32[]{:S(2)}) async-start(), calls=%async_computation.10 | async-start | bytes 1327104
  205.0 2.0 copy-start.14
  205.0 2.0 copy-start.32
  205.0 2.0 copy-start.39
  209.2 38.7 %copy-start.33 = (bf16[512,768]{1,0:T(8,128)(2,1)S(1)}, bf16[512,768]{1,0:T(8,128)(2,1)}, u32[]{:S(2)}) copy-start(bf16[512,768]{1,0:T(8,128)(2,1)} %param.21) | copy-start | bytes 2359300
  209.3 38.6 %copy-start.40 = (bf16[512,768]{1,0:T(8,128)(2,1)S(1)}, bf16[512,768]{1,0:T(8,128)(2,1)}, u32[]{:S(2)}) copy-start(bf16[512,768]{1,0:T(8,128)(2,1)} %all-reduce.7.cloned.1.call-done) | copy-start | bytes 2359300
  210.7 39.2 %copy-start.37 = (f32[512,768]{1,0:T(8,128)S(1)}, f32[512,768]{1,0:T(8,128)}, u32[]{:S(2)}) copy-start(f32[512,768]{1,0:T(8,128)} %copy-done.36) | copy-start | bytes 4718596
  210.8 148.8 %all-reduce.15.cloned.1.call-start = ((), (), s32[]{:S(2)}) async-start(), calls=%async_computation.12 | async-start | bytes 3145728 | tf_op jit(solution)/shard_map/psum | solution.py:436
  247.9 2.0 copy-start.46
  249.9 1.7 copy-start.51
  252.8 4.7 copy-start.62
  260.2 138.8 %reduce-scatter.13.cloned.1.call-start = ((), (), s32[]{:S(2)}) async-start(), calls=%async_computation.9 | async-start | bytes 1327104
  262.6 1.8 copy-start.42
  262.6 1.8 copy-start.55
  264.2 180.7 %reduce-scatter.17.cloned.1.call-start = ((), (), s32[]{:S(2)}) async-start(), calls=%async_computation.11 | async-start | bytes 2654208
  265.1 1.8 copy-start.53
  265.1 1.8 copy-start.74
  270.3 2.3 copy-start.7
  270.3 237.3 %reduce-scatter.11.cloned.1.call-start = ((), (), s32[]{:S(2)}) async-start(), calls=%async_computation.8 | async-start | bytes 3932160 | tf_op jit(solution)/shard_map/reduce_scatter | solution.py:445
  288.3 97.5 %copy-start.29 = (f32[512,768]{1,0:T(8,128)S(1)}, f32[512,768]{1,0:T(8,128)}, u32[]{:S(2)}) copy-start(f32[512,768]{1,0:T(8,128)} %copy-done.27) | copy-start | bytes 4718596
  359.6 26.1 %copy-start.43 = (bf16[512,768]{1,0:T(8,128)(2,1)S(1)}, bf16[512,768]{1,0:T(8,128)(2,1)}, u32[]{:S(2)}) copy-start(bf16[512,768]{1,0:T(8,128)(2,1)} %get-tuple-element.129) | copy-start | bytes 2359300
  447.9 62.2 %copy-start.1 = (bf16[2048,768]{1,0:T(8,128)(2,1)S(1)}, bf16[2048,768]{1,0:T(8,128)(2,1)}, u32[]{:S(2)}) copy-start(bf16[2048,768]{1,0:T(8,128)(2,1)} %param.22) | copy-start | bytes 9437188
  (36 other events, 41.1 us)
Sparse Core Ops, SparseCore 0:
  25.4 46.3 all-reduce.6
  81.8 42.9 all-reduce.8
  136.2 42.9 all-reduce.10
  204.9 42.9 all-reduce.12
  251.0 36.1 reduce-scatter.14
  290.1 69.4 all-reduce.14
  363.2 35.8 reduce-scatter.12
  402.4 42.4 reduce-scatter.16
  447.3 60.2 reduce-scatter.10
